TPU v7x, 32 devices: a whole 2x2x4 slice. The times are simulated.
32 devices in a mesh: groups: 1, sample: 32 (over z, y, x, core).
Axes of the slice: x: 2, y: 2, z: 4, core: 2. Of those that a mesh axis runs over, the one named last changes fastest.
Arguments:
- hidden: bfloat16 [32, 256, 14336], P(('groups', 'sample')), may hold values from -6 to 6
- cotangent: bfloat16 [32, 256, 4096], P(('groups', 'sample')), may hold values from -6 to 6
- loss_mask: int32 [32, 256], P(('groups', 'sample')), may hold values 0 or 1
- project_hidden: bfloat16 [14336, 64], replicated, may hold values from -0.046875 to 0.046875
- project_model: bfloat16 [4096, 64], replicated, may hold values from -0.09375 to 0.09375
- queries: int32 [32], P('groups'), may hold values from 0 to 31, as said below
Outputs:
- projected: float32 [32, 4096], P(('groups', 'sample'))
- scores: float32 [32, 32], P(('groups', 'sample'))
Inputs may be any that keep to these rules, and one draw needn't show every extreme that they name: `queries`: 32 distinct indices; the last sequence of the block is always among them.
All inputs are finite; a program needn't handle non-finite values. No bound on the sum of `loss_mask` on one device may be relied on, other than what follows from the above.
Results may differ from a plain program's by a relative error of at most 0.0003.
Values sent between devices are 32-bit elements; how exact they have to be, the bound alone decides.
A program may use at most 64 MiB of HBM per device.

v0:
```python
import jax
import jax.numpy as jnp
from jax import lax
from jax.sharding import PartitionSpec as P


def damp(factor, counted, rank):
    mean = factor / jnp.maximum(counted, 1.0)
    lam = 0.1 * jnp.trace(mean) / rank + 1e-06
    return mean + lam * jnp.eye(rank, dtype=jnp.float32)


def precondition(damped_in, damped_out, query_grads, rank):
    nquery = query_grads.shape[0]
    lower_in = jnp.linalg.cholesky(damped_in)
    lower_out = jnp.linalg.cholesky(damped_out)
    stacked = jnp.transpose(query_grads, (1, 0, 2)).reshape(rank, nquery * rank)
    left = jax.scipy.linalg.cho_solve((lower_in, True), stacked)
    flipped = jnp.transpose(left.reshape(rank, nquery, rank), (2, 1, 0)).reshape(
        rank, nquery * rank
    )
    right = jax.scipy.linalg.cho_solve((lower_out, True), flipped)
    return jnp.transpose(right.reshape(rank, nquery, rank), (1, 2, 0)).reshape(nquery, rank * rank)


def pick_rows(queries, everyone):
    picker = (queries[:, None] == jnp.arange(everyone.shape[0], dtype=jnp.int32)[None, :]).astype(
        jnp.float32
    )
    return jnp.dot(picker, everyone, precision=lax.Precision.HIGHEST)


def local(hidden, cotangent, loss_mask, project_hidden, project_model, queries):
    count_seq = hidden.shape[0]
    seq_len = hidden.shape[1]
    rank = project_hidden.shape[1]
    nquery = queries.shape[0]
    hidden_low = jnp.dot(
        hidden.reshape(count_seq * seq_len, hidden.shape[2]),
        project_hidden,
        preferred_element_type=jnp.float32,
    ).reshape(count_seq, seq_len, rank)
    maskf = loss_mask.astype(jnp.float32)[:, :, None]
    weighted = (
        jnp.dot(
            cotangent.reshape(count_seq * seq_len, cotangent.shape[2]),
            project_model,
            preferred_element_type=jnp.float32,
        ).reshape(count_seq, seq_len, rank)
        * maskf
    )
    grads = jnp.einsum(
        "str,stk->srk", hidden_low, weighted, precision=lax.Precision.HIGHEST
    ) / jnp.sqrt(jnp.float32(seq_len))
    grads = grads.reshape(count_seq, rank * rank)
    local_in = jnp.einsum(
        "str,stk->rk", hidden_low * maskf, hidden_low, precision=lax.Precision.HIGHEST
    )
    local_out = jnp.einsum("str,stk->rk", weighted, weighted, precision=lax.Precision.HIGHEST)
    local_count = jnp.sum(maskf)
    factor_in, factor_out, counted = lax.psum((local_in, local_out, local_count), "sample")
    everyone = lax.all_gather(grads, "sample", axis=0, tiled=True)
    chosen = pick_rows(queries, everyone)
    damped_in = damp(factor_in, counted, rank)
    damped_out = damp(factor_out, counted, rank)
    precond = precondition(damped_in, damped_out, chosen.reshape(nquery, rank, rank), rank)
    scores = jnp.dot(grads, precond.T, precision=lax.Precision.HIGHEST) / rank
    return (grads, scores)


def solution(mesh):
    in_specs = (
        P(("groups", "sample"), None, None),
        P(("groups", "sample"), None, None),
        P(("groups", "sample"), None),
        P(),
        P(),
        P("groups"),
    )
    out_specs = (P(("groups", "sample"), None), P(("groups", "sample"), None))
    return jax.shard_map(local, mesh=mesh, in_specs=in_specs, out_specs=out_specs, check_vma=False)
```

profile of v0, /device:TPU:1, one launch (start us, length us, event | category | flops | bytes accessed | tf_op | source)
XLA Modules:
  0.0 139.8 jit_solution(2532342149571208195)
XLA Ops:
  0.6 0.0 copy-start
  0.6 0.0 copy-start.2
  0.7 0.0 copy-start.1
  0.7 6.1 %fusion = f32[256,64]{0,1:T(8,128)S(1)} fusion(bf16[14336,64]{0,1:T(8,128)(2,1)} %param.12, bf16[1,256,14336]{2,1,0:T(8,128)(2,1)} %param.9), kind=kOutput, calls=%fused_computation | convolution fusion | flops 469762048 | bytes 9240576 | tf_op jit(solution)/shard_map/dot_general | solution.py:38
  6.7 0.0 copy-done.2
  6.8 0.2 fusion.13
  7.0 0.0 copy-done
  7.0 0.0 copy-done.1
  7.0 0.0 copy-start.3
  7.0 0.8 fusion.4
  7.8 0.2 fusion.29
  8.0 0.6 convert_reduce_fusion
  8.6 41.4 %all-reduce = (f32[64,64]{0,1:T(8,128)S(1)}, f32[]{:T(128)}, f32[64,64]{0,1:T(8,128)S(1)}) all-reduce(f32[64,64]{0,1:T(8,128)S(1)} %fusion.13, f32[]{:T(128)} %convert_reduce_fusion, f32[64,64]{0,1:T(8,128)S(1)} %fusion.29), channel_id=1, replica_groups=mesh['groups'=1,'sample'=32] {'sample'}, use_global_device_ids=true, to_apply=%region_6.8 | all-reduce | flops 8193 | bytes 65544 | tf_op jit(solution)/shard_map/psum | solution.py:61
  50.6 0.6 select_reduce_fusion.3
  51.9 0.6 select_reduce_fusion.2
  53.2 0.1 copy.19
  53.3 5.8 %cholesky.44 = f32[64,64]{1,0:T(8,128)S(1)} custom-call(f32[64,64]{1,0:T(8,128)S(1)} %fusion.26), custom_call_target="Cholesky" | custom-call | tf_op jit(solution)/shard_map/jit(cholesky)/cholesky | solution.py:16
  59.2 0.6 compare_reduce_fusion.1
  59.8 0.7 fusion.15
  60.5 4.9 %custom-call.9 = f32[1,64,64]{1,2,0:T(8,128)S(1)} custom-call(f32[1,64,64]{2,1,0:T(8,128)S(1)} %fusion.15), custom_call_target="InvertDiagBlocksLowerTriangular" | custom-call | tf_op jit(solution)/shard_map/jit(_cho_solve)/triangular_solve | solution.py:22
  65.4 0.1 copy.21
  65.5 5.8 %cholesky.55 = f32[64,64]{1,0:T(8,128)S(1)} custom-call(f32[64,64]{1,0:T(8,128)S(1)} %fusion.21), custom_call_target="Cholesky" | custom-call | tf_op jit(solution)/shard_map/jit(cholesky)/cholesky | solution.py:15
  71.4 0.6 compare_reduce_fusion
  72.0 0.7 fusion.16
  72.7 4.9 %custom-call.8 = f32[1,64,64]{1,2,0:T(8,128)S(1)} custom-call(f32[1,64,64]{2,1,0:T(8,128)S(1)} %fusion.16), custom_call_target="InvertDiagBlocksLowerTriangular" | custom-call | tf_op jit(solution)/shard_map/jit(_cho_solve)/triangular_solve | solution.py:18
  77.6 0.2 convolution_multiply_fusion
  77.8 0.1 reshape.74
  77.9 43.1 %all-gather = f32[32,1,4096]{2,1,0:T(1,128)S(1)} all-gather(f32[1,1,4096]{2,1,0:T(1,128)S(1)} %reshape.74), channel_id=1, replica_groups=mesh['groups'=1,'sample'=32] {'sample'}, dimensions={0}, use_global_device_ids=true | all-gather | bytes 540672 | tf_op jit(solution)/shard_map/all_gather | solution.py:62
  121.0 0.0 copy-done.3
  121.0 1.5 %fusion.10 = f32[32,4096]{1,0:T(8,128)} fusion(f32[32,1,4096]{2,1,0:T(1,128)S(1)} %all-gather, s32[32]{0:T(128)S(1)} %copy-done.3), kind=kOutput, calls=%fused_computation.11 | convolution fusion | flops 50332672 | bytes 1048704 | tf_op jit(solution)/shard_map/dot_general | solution.py:30
  122.5 1.5 %reshape.69 = f32[32,64,64]{2,1,0:T(8,128)S(1)} reshape(f32[32,4096]{1,0:T(8,128)} %fusion.10) | data formatting | bytes 1048576 | tf_op jit(solution)/shard_map/reshape | solution.py:66
  124.0 1.6 %copy.33 = f32[32,64,64]{2,0,1:T(8,128)} copy(f32[32,64,64]{2,1,0:T(8,128)S(1)} %reshape.69) | data formatting | bytes 1048576 | tf_op jit(solution)/shard_map/reshape | solution.py:66
  125.6 1.6 %reshape.70 = f32[64,2048]{1,0:T(8,128)S(1)} reshape(f32[64,32,64]{2,1,0:T(8,128)} %bitcast.62) | data formatting | bytes 1048576 | tf_op jit(solution)/shard_map/reshape | solution.py:17
  127.1 0.6 fusion.19
  127.8 1.4 fusion.17
  129.1 1.5 %reshape.71 = f32[64,32,64]{2,1,0:T(8,128)S(1)} reshape(f32[64,2048]{1,0:T(8,128)} %fusion.17) | data formatting | bytes 1048576 | tf_op jit(solution)/shard_map/reshape | solution.py:19
  130.6 2.0 %copy.23 = f32[64,32,64]{0,1,2:T(8,128)} copy(f32[64,32,64]{2,1,0:T(8,128)S(1)} %reshape.71) | data formatting | bytes 1048576 | tf_op jit(solution)/shard_map/reshape | solution.py:19
  132.6 1.6 %reshape.72 = f32[64,2048]{1,0:T(8,128)S(1)} reshape(f32[64,32,64]{2,1,0:T(8,128)} %bitcast.63) | data formatting | bytes 1048576 | tf_op jit(solution)/shard_map/reshape | solution.py:19
  134.2 0.6 fusion.24
  134.8 1.4 fusion.22
  136.2 1.5 %reshape.73 = f32[64,32,64]{2,1,0:T(8,128)S(1)} reshape(f32[64,2048]{1,0:T(8,128)} %fusion.22) | data formatting | bytes 1048576 | tf_op jit(solution)/shard_map/reshape | solution.py:23
  137.6 0.1 copy.26
  137.7 1.5 %fusion.8 = f32[1,32]{1,0:T(1,128)} fusion(f32[64,64,1]{0,2,1:T(1,128)S(1)} %copy.26, f32[64,32,64]{2,1,0:T(8,128)S(1)} %reshape.73), kind=kOutput, calls=%fused_computation.8 | convolution fusion | flops 1572896 | bytes 540800 | tf_op jit(solution)/shard_map/dot_general | solution.py:67
  139.2 0.7 reshape.68
  (6 shorter events, 0.1 us)
Async XLA Ops:
  0.6 6.4 %copy-start = (bf16[1,256,4096]{2,1,0:T(8,128)(2,1)S(1)}, bf16[1,256,4096]{2,1,0:T(8,128)(2,1)}, u32[]{:S(2)}) copy-start(bf16[1,256,4096]{2,1,0:T(8,128)(2,1)} %param.10) | copy-start | bytes 6291460
  0.6 6.1 %copy-start.2 = (s32[1,256]{1,0:T(1,128)S(1)}, s32[1,256]{1,0:T(1,128)}, u32[]{:S(2)}) copy-start(s32[1,256]{1,0:T(1,128)} %param.11) | copy-start | bytes 3076
  0.7 6.3 %copy-start.1 = (bf16[4096,64]{0,1:T(8,128)(2,1)S(1)}, bf16[4096,64]{0,1:T(8,128)(2,1)}, u32[]{:S(2)}) copy-start(bf16[4096,64]{0,1:T(8,128)(2,1)} %param.13) | copy-start | bytes 1572868
  7.0 114.0 %copy-start.3 = (s32[32]{0:T(128)S(1)}, s32[32]{0:T(128)}, u32[]{:S(2)}) copy-start(s32[32]{0:T(128)} %param.14) | copy-start | bytes 388
where the time goes:
time: 140 us
  blocking collectives  84.5 us (60%)
  other arithmetic  26 us (19%)
  matrix products  14.4 us (10%)
  local copies, waits for them, and re-layouts  12.2 us (9%)
  between operations  2.79 us (2%)
    all_gather x1, blocking collectives, local(): everyone = lax.all_gather(grads, 'sample', axis=0, tiled=True)  43.1 us
    psum x1, blocking collectives, local(): lax.psum((local_in, local_out, local_count), 'sample')  41.4 us
    another operation x3, other arithmetic, precondition(): lower_out = jnp.linalg.cholesky(damped_out)  6.52 us
    another operation x3, other arithmetic, precondition(): lower_in = jnp.linalg.cholesky(damped_in)  6.52 us
    dot_general x1, matrix products, local(): jnp.dot(hidden.reshape(count_seq * seq_len, hidden.shape[2]), project_hid...  6.08 us
    another operation x2, other arithmetic, precondition(): right = jax.scipy.linalg.cho_solve((lower_out, True), flipped)  5.55 us
    another operation x2, other arithmetic, precondition(): left = jax.scipy.linalg.cho_solve((lower_in, True), stacked)  5.55 us
    reshape x2, local copies, waits for them, and re-layouts, precondition(): left.reshape(rank, nquery, rank)  3.45 us

commit v1 on v0

v1 whole, which is shorter than its diff:
```python
import functools

import jax
import jax.numpy as jnp
from jax import lax
from jax.experimental import pallas as pl
from jax.experimental.pallas import tpu as pltpu
from jax.sharding import PartitionSpec as P

MESH = pl.DeviceIdType.MESH
HIGHEST = lax.Precision.HIGHEST
PLANE = 8
NT = (((1,), (1,)), ((), ()))
SQUARINGS = 7


def exact(a, b):
    return jnp.dot(a, b, precision=HIGHEST, preferred_element_type=jnp.float32)


def inverses(factors):
    rank = factors.shape[0]
    row = lax.broadcasted_iota(jnp.int32, factors.shape, 0)
    lane = lax.broadcasted_iota(jnp.int32, factors.shape, 1)
    first = lane < rank
    diagonal = row == jnp.where(first, lane, lane - rank)

    def both(values):
        one = jnp.sum(jnp.where(first, values, 0.0), keepdims=True)
        two = jnp.sum(jnp.where(first, 0.0, values), keepdims=True)
        lane1 = lax.broadcasted_iota(jnp.int32, (1, 2 * rank), 1)
        return jnp.where(lane1 < rank, one, two)

    trace = both(jnp.where(diagonal, factors, 0.0))
    frob = jnp.sqrt(both(factors * factors))
    lam = 0.1 * trace / rank + 1e-06
    low, high = lam, lam + jnp.minimum(trace, frob) * 1.0001
    damped = jnp.where(diagonal, factors + lam, factors)

    def blocks(values):
        return jnp.concatenate(
            [jnp.where(first, values, 0.0), jnp.where(first, 0.0, values)], axis=0
        )

    eye = blocks(jnp.where(diagonal, 1.0, 0.0))
    damped = blocks(damped)
    scale = 2.0 / (low + high)
    rho = (high - low) / (high + low)
    x = eye * scale
    r = eye - damped * scale
    for _ in range(SQUARINGS):
        c = 2.0 / (2.0 - rho * rho)
        product = exact(jnp.concatenate([r, x], axis=0), r)
        x = (x + product[2 * rank :]) * c
        r = (1.0 - c) * eye + product[: 2 * rank] * c
        rho = rho * rho / (2.0 - rho * rho)
        yield None
    x = x + exact(x, eye - exact(damped, x))
    yield x


def kernel(
    n, chunks_h, chunks_c,
    hidden, cot, mask, proj_h, proj_m, queries,
    grads_out, scores_out,
    h_v, c_v, ph_v, pm_v, pair, fac, rs, red, zr, fs, g,
    in_sem, rs_send, rs_recv, z_send, z_recv, ag_send, ag_recv, g_send, g_recv,
):
    seq, ff = h_v.shape
    d = c_v.shape[1]
    rank = ph_v.shape[0]
    me = lax.axis_index("sample")
    high = n // PLANE
    hi, low = me // PLANE, me % PLANE

    def in_plane(t):
        return hi * PLANE + (low + t) % PLANE

    def in_column(t):
        return (hi + t) % high * PLANE + low

    loads = []
    step = d // chunks_c
    for i in range(chunks_c):
        cols = pl.ds(i * step, step)
        loads.append([(cot.at[0, :, cols], c_v.at[:, cols]), (proj_m.at[:, cols], pm_v.at[:, cols])])
    step = ff // chunks_h
    for i in range(chunks_h):
        cols = pl.ds(i * step, step)
        loads.append([(hidden.at[0, :, cols], h_v.at[:, cols]), (proj_h.at[:, cols], ph_v.at[:, cols])])
    copies = []
    for i, two in enumerate(loads):
        copies.append(
            [pltpu.make_async_copy(src, dst, in_sem.at[2 * i + j]) for j, (src, dst) in enumerate(two)]
        )
        for copy in copies[-1]:
            copy.start()

    barrier = pltpu.get_barrier_semaphore()
    partners = [in_plane(t) for t in range(1, PLANE)] + [in_column(t) for t in range(1, high)]
    for partner in partners:
        pl.semaphore_signal(barrier, inc=1, device_id={"sample": partner}, device_id_type=MESH)

    weighted = jnp.zeros((rank, seq), jnp.float32)
    step = d // chunks_c
    for i in range(chunks_c):
        for copy in copies[i]:
            copy.wait()
        cols = pl.ds(i * step, step)
        weighted += lax.dot_general(pm_v[:, cols], c_v[:, cols], NT, preferred_element_type=jnp.float32)
    hidden_low = jnp.zeros((rank, seq), jnp.float32)
    step = ff // chunks_h
    for i in range(chunks_h):
        for copy in copies[chunks_c + i]:
            copy.wait()
        cols = pl.ds(i * step, step)
        hidden_low += lax.dot_general(ph_v[:, cols], h_v[:, cols], NT, preferred_element_type=jnp.float32)

    maskf = mask[...].astype(jnp.float32)
    both = jnp.concatenate([hidden_low, weighted], axis=0) * maskf
    gram = lax.dot_general(both, both, NT, precision=HIGHEST, preferred_element_type=jnp.float32)
    row = lax.broadcasted_iota(jnp.int32, (rank, 2 * rank), 0)
    lane = lax.broadcasted_iota(jnp.int32, (rank, 2 * rank), 1)
    first = lane < rank
    factors = jnp.where(first, gram[:rank], gram[rank:])
    spare = (row == 1) & (lane == 0)
    count = jnp.sum(maskf, keepdims=True)
    fac[...] = jnp.where(spare, count, factors).reshape(fac.shape)

    pl.semaphore_wait(barrier, len(partners))

    def remote(src, dst, send, recv, partner):
        return pltpu.make_async_remote_copy(
            src_ref=src, dst_ref=dst, send_sem=send, recv_sem=recv,
            device_id={"sample": partner}, device_id_type=MESH,
        )

    started = []

    def start(copies):
        for copy in copies:
            copy.start()
        started.extend(copies)
        return copies

    to_plane = start([
        remote(fac.at[(low + t) % PLANE], rs.at[t - 1], rs_send.at[t - 1], rs_recv.at[t - 1], in_plane(t))
        for t in range(1, PLANE)
    ])

    grad = jnp.where(first, 0.0, gram[:rank]) * (1.0 / seq**0.5)
    twice = grad + pltpu.roll(grad, rank, 1)
    half = rank // 2
    place = hi + high * ((low // 4) % 2) + 2 * high * ((low // 2) % 2) + 4 * high * (low % 2)
    g[place] = jnp.where(first[:half], twice[:half], twice[half:])

    def g_copies(stage):
        if stage == 0:
            return [
                remote(g.at[place], g.at[place], g_send.at[t - 1], g_recv.at[t - 1], in_column(t))
                for t in range(1, high)
            ]
        held = high * 2 ** (stage - 1)
        bit = PLANE // 2**stage
        partner = me + (1 - 2 * ((me // bit) % 2)) * bit
        span = pl.ds(pl.multiple_of(place // held * held, held), held)
        sem = high - 2 + stage
        return [remote(g.at[span], g.at[span], g_send.at[sem], g_recv.at[sem], partner)]

    stages = [start(g_copies(0))]

    def next_stage():
        for copy in stages[-1]:
            copy.wait_recv()
        if len(stages) < 4:
            stages.append(start(g_copies(len(stages))))

    pair[...] = twice
    grads_out[...] = jnp.where(
        first[:half], pair[pl.ds(0, half, stride=2), :], pair[pl.ds(1, half, stride=2), :]
    )

    for copy in to_plane:
        copy.wait_recv()
    part = fac[low]
    for t in range(PLANE - 1):
        part += rs[t]
    red[...] = part
    to_column = start([
        remote(red, zr.at[t - 1], z_send.at[t - 1], z_recv.at[t - 1], in_column(t))
        for t in range(1, high)
    ])
    next_stage()
    for copy in to_column:
        copy.wait_recv()
    for t in range(high - 1):
        part += zr[t]
    fs[low] = part
    shares = start([
        remote(fs.at[low], fs.at[low], ag_send.at[t - 1], ag_recv.at[t - 1], in_plane(t))
        for t in range(1, PLANE)
    ])
    for copy in shares:
        copy.wait_recv()
    next_stage()
    total = fs[...].reshape(rank, 2 * rank)
    counted = jnp.maximum(jnp.sum(jnp.where(spare, total, 0.0), keepdims=True), 1.0)
    twin = jnp.sum(jnp.where((row == 0) & (lane == 1), total, 0.0), keepdims=True)
    total = jnp.where(spare, twin, total)
    for i, inverse in enumerate(inverses(total / counted)):
        if i == 2:
            next_stage()

    zeros = jnp.zeros((rank, 2 * rank), jnp.float32)
    left = exact(inverse, jnp.concatenate([grad, zeros], axis=0))
    precond = exact(left[:rank], inverse) * (1.0 / rank)
    precond = precond + pltpu.roll(precond, rank, 1)
    precond = jnp.where(first[:half], precond[:half], precond[half:])
    next_stage()
    terms = g[...] * precond[None]
    terms = jnp.sum(terms.reshape(n, half // 8, 8, 2 * rank), axis=1).reshape(n * 8, 2 * rank)
    sums = jnp.sum(terms, axis=1, keepdims=True)
    nquery = scores_out.shape[1]
    at = lax.broadcasted_iota(jnp.int32, (n * 8, nquery), 0) // 8
    index = at % high * 8 + at // high % 2 * 4 + at // (2 * high) % 2 * 2 + at // (4 * high)
    scores_out[...] = jnp.sum(jnp.where(index == queries[...], sums, 0.0), axis=0, keepdims=True)
    for copy in started:
        copy.wait_send()


def local(n, hidden, cotangent, loss_mask, project_hidden, project_model, queries):
    _, seq, ff = hidden.shape
    d = cotangent.shape[2]
    rank = project_hidden.shape[1]
    nquery = queries.shape[0]
    high = n // PLANE
    chunks_h, chunks_c = 7, 2
    vmem = pl.BlockSpec(memory_space=pltpu.VMEM)
    hbm = pl.BlockSpec(memory_space=pl.ANY)
    sem = pltpu.SemaphoreType.DMA
    f32 = jnp.float32
    rows = rank // PLANE
    grads, scores = pl.pallas_call(
        functools.partial(kernel, n, chunks_h, chunks_c),
        out_shape=(
            jax.ShapeDtypeStruct((rank // 2, 2 * rank), f32),
            jax.ShapeDtypeStruct((1, nquery), f32),
        ),
        in_specs=[hbm, hbm, vmem, hbm, hbm, vmem],
        out_specs=(vmem, vmem),
        scratch_shapes=[
            pltpu.VMEM((seq, ff), jnp.bfloat16),
            pltpu.VMEM((seq, d), jnp.bfloat16),
            pltpu.VMEM((rank, ff), jnp.bfloat16),
            pltpu.VMEM((rank, d), jnp.bfloat16),
            pltpu.VMEM((rank, 2 * rank), f32),
            pltpu.VMEM((PLANE, rows, 2 * rank), f32),
            pltpu.VMEM((PLANE - 1, rows, 2 * rank), f32),
            pltpu.VMEM((rows, 2 * rank), f32),
            pltpu.VMEM((high - 1, rows, 2 * rank), f32),
            pltpu.VMEM((PLANE, rows, 2 * rank), f32),
            pltpu.VMEM((n, rank // 2, 2 * rank), f32),
            sem((2 * (chunks_h + chunks_c),)),
            sem((PLANE - 1,)),
            sem((PLANE - 1,)),
            sem((high - 1,)),
            sem((high - 1,)),
            sem((PLANE - 1,)),
            sem((PLANE - 1,)),
            sem((high + 2,)),
            sem((high + 2,)),
        ],
        compiler_params=pltpu.CompilerParams(
            collective_id=0, has_side_effects=True, vmem_limit_bytes=48 * 2**20
        ),
    )(hidden, cotangent, loss_mask, project_hidden.T, project_model.T, queries.reshape(1, nquery))
    return grads.reshape(1, rank * rank), scores


def solution(mesh):
    in_specs = (
        P(("groups", "sample"), None, None),
        P(("groups", "sample"), None, None),
        P(("groups", "sample"), None),
        P(),
        P(),
        P("groups"),
    )
    out_specs = (P(("groups", "sample"), None), P(("groups", "sample"), None))
    return jax.shard_map(
        functools.partial(local, mesh.shape["sample"]),
        mesh=mesh, in_specs=in_specs, out_specs=out_specs, check_vma=False,
    )
```

time: 140 us -> 35.4 us (0.25)
  blocking collectives: 84.5 us -> 0 us
  Pallas kernels: 0 us -> 28 us
  other arithmetic: 26 us -> 0 us
  matrix products: 14.4 us -> 0 us
  local copies, waits for them, and re-layouts: 12.2 us -> 6.58 us
  between operations: 2.79 us -> 0.65 us
    all_gather x1 -> x0, blocking collectives: 43.1 us -> none  [local(): everyone = lax.all_gather(grads, 'sample', axis=0, tiled=True)]
    psum x1 -> x0, blocking collectives: 41.4 us -> none  [local(): lax.psum((local_in, local_out, local_count), 'sample')]
    pallas_call x0 -> x1, Pallas kernels: none -> 28 us  [local(): pl.pallas_call(functools.partial(kernel, n, chunks_h, chunks_c), out_shap...]
    another operation x10 -> x0, other arithmetic: 24.1 us -> none  [the longest x3 6.52 us: precondition(): lower_out = jnp.linalg.cholesky(damped_out)]
    reshape x8 -> x0, local copies, waits for them, and re-layouts: 11.8 us -> none  [the longest x2 3.45 us: precondition(): left.reshape(rank, nquery, rank)]
    dot_general x7 -> x0, matrix products: 10.4 us -> none  [the longest x1 6.08 us: local(): jnp.dot(hidden.reshape(count_seq * seq_len, hidden.shape[2]), project_hid...]
    unnamed x9 -> x12, local copies, waits for them, and re-layouts: 0.11 us -> 6.58 us
    another operation x4 -> x0, matrix products: 3.97 us -> none  [the longest x2 1.99 us: precondition(): left = jax.scipy.linalg.cho_solve((lower_in, True), stacked)]
where the time goes in v1:
time: 35.4 us; the launch traced here: 35.2 us
  Pallas kernels  28 us (79%)
  local copies, waits for them, and re-layouts  6.58 us (19%)
  between operations  0.65 us (2%)
    pallas_call x1, Pallas kernels, local(): pl.pallas_call(functools.partial(kernel, n, chunks_h, chunks_c), out_shap...  28 us
    unnamed x12, local copies, waits for them, and re-layouts  6.58 us

profile of v1, /device:TPU:1, one launch (start us, length us, event | category | flops | bytes accessed | tf_op | source)
XLA Modules:
  0.0 35.2 jit_solution(9144397530994473314)
XLA Ops:
  0.6 0.0 copy-start
  0.6 1.6 %copy-done = bf16[1,256,4096]{2,1,0:T(8,128)(2,1)S(1)} copy-done((bf16[1,256,4096]{2,1,0:T(8,128)(2,1)S(1)}, bf16[1,256,4096]{2,1,0:T(8,128)(2,1)}, u32[]{:S(2)}) %copy-start) | copy-done | bytes 2097176
  2.2 0.0 copy-start.1
  2.2 1.5 %copy-done.1 = bf16[14336,64]{0,1:T(8,128)(2,1)S(1)} copy-done((bf16[14336,64]{0,1:T(8,128)(2,1)S(1)}, bf16[14336,64]{0,1:T(8,128)(2,1)}, u32[]{:S(2)}) %copy-start.1) | copy-done | bytes 1835032
  3.7 0.0 copy-start.2
  3.7 1.0 %copy-done.2 = bf16[4096,64]{0,1:T(8,128)(2,1)S(1)} copy-done((bf16[4096,64]{0,1:T(8,128)(2,1)S(1)}, bf16[4096,64]{0,1:T(8,128)(2,1)}, u32[]{:S(2)}) %copy-start.2) | copy-done | bytes 524312
  4.8 0.0 copy-start.3
  4.8 0.7 %copy-done.3 = s32[1,256]{1,0:T(1,128)S(1)} copy-done((s32[1,256]{1,0:T(1,128)S(1)}, s32[1,256]{1,0:T(1,128)}, u32[]{:S(2)}) %copy-start.3) | copy-done | bytes 1048
  5.4 0.0 copy-start.4
  5.4 0.7 %copy-done.4 = s32[32]{0:T(128)S(1)} copy-done((s32[32]{0:T(128)S(1)}, s32[32]{0:T(128)}, u32[]{:S(2)}) %copy-start.4) | copy-done | bytes 152
  6.1 28.0 %shard_map.77 = (f32[32,128]{1,0:T(8,128)S(1)}, f32[1,32]{1,0:T(1,128)S(1)}) custom-call(bf16[1,256,14336]{2,1,0:T(8,128)(2,1)} %hidden.1, bf16[1,256,4096]{2,1,0:T(8,128)(2,1)S(1)} %copy-done, s32[1,256]{1,0:T(1,128)S(1)} %copy-done.3, bf16[64,14336]{1,0:T(8,128)(2,1)S(1)} %bitcast.4, bf16[64,4096]{1,0:T(8,128)(2,1)S(1)} %bitcast.5, s32[1,32]{1,0:T(1,128)S(1)} %bitcast.7), custom_call_target="tpu_custom_call" | custom-call | tf_op jit(solution)/shard_map/pallas_call | solution.py:243
  34.1 0.6 %copy.10 = f32[1,4096]{1,0:T(1,128)} copy(f32[1,4096]{1,0:T(1,128)S(1)} %bitcast.6) | data formatting | bytes 32768
  34.7 0.5 %copy.11 = f32[1,32]{1,0:T(1,128)} copy(f32[1,32]{1,0:T(1,128)S(1)} %get-tuple-element.9) | data formatting | bytes 256
Async XLA Ops:
  0.6 1.6 %copy-start = (bf16[1,256,4096]{2,1,0:T(8,128)(2,1)S(1)}, bf16[1,256,4096]{2,1,0:T(8,128)(2,1)}, u32[]{:S(2)}) copy-start(bf16[1,256,4096]{2,1,0:T(8,128)(2,1)} %cot.1) | copy-start | bytes 6291460
  2.2 1.5 %copy-start.1 = (bf16[14336,64]{0,1:T(8,128)(2,1)S(1)}, bf16[14336,64]{0,1:T(8,128)(2,1)}, u32[]{:S(2)}) copy-start(bf16[14336,64]{0,1:T(8,128)(2,1)} %param.9) | copy-start | bytes 5505028
  3.7 1.0 %copy-start.2 = (bf16[4096,64]{0,1:T(8,128)(2,1)S(1)}, bf16[4096,64]{0,1:T(8,128)(2,1)}, u32[]{:S(2)}) copy-start(bf16[4096,64]{0,1:T(8,128)(2,1)} %param.10) | copy-start | bytes 1572868
  4.8 0.7 %copy-start.3 = (s32[1,256]{1,0:T(1,128)S(1)}, s32[1,256]{1,0:T(1,128)}, u32[]{:S(2)}) copy-start(s32[1,256]{1,0:T(1,128)} %mask.1) | copy-start | bytes 3076
  5.4 0.7 %copy-start.4 = (s32[32]{0:T(128)S(1)}, s32[32]{0:T(128)}, u32[]{:S(2)}) copy-start(s32[32]{0:T(128)} %param.11) | copy-start | bytes 388

commit v2 on v1

--- a/solution.py
+++ b/solution.py
@@ -12,6 +12,7 @@
 PLANE = 8
 NT = (((1,), (1,)), ((), ()))
 SQUARINGS = 7
+AHEAD = 4
 
 
 def exact(a, b):
@@ -63,7 +64,7 @@
     n, chunks_h, chunks_c,
     hidden, cot, mask, proj_h, proj_m, queries,
     grads_out, scores_out,
-    h_v, c_v, ph_v, pm_v, pair, fac, rs, red, zr, fs, g,
+    h_v, c_v, ph_v, pm_v, m_v, q_v, pair, fac, rs, red, zr, fs, g_a, g_b,
     in_sem, rs_send, rs_recv, z_send, z_recv, ag_send, ag_recv, g_send, g_recv,
 ):
     seq, ff = h_v.shape
@@ -93,8 +94,24 @@
         copies.append(
             [pltpu.make_async_copy(src, dst, in_sem.at[2 * i + j]) for j, (src, dst) in enumerate(two)]
         )
-        for copy in copies[-1]:
+    small = [
+        pltpu.make_async_copy(mask, m_v, in_sem.at[2 * len(loads)]),
+        pltpu.make_async_copy(queries, q_v, in_sem.at[2 * len(loads) + 1]),
+    ]
+
+    def fetch(i):
+        for copy in copies[i] if i < len(loads) else ():
             copy.start()
+
+    def arrived(i):
+        for copy in copies[i]:
+            copy.wait()
+        fetch(i + AHEAD)
+
+    for i in range(AHEAD):
+        fetch(i)
+    for copy in small:
+        copy.start()
 
     barrier = pltpu.get_barrier_semaphore()
     partners = [in_plane(t) for t in range(1, PLANE)] + [in_column(t) for t in range(1, high)]
@@ -104,19 +121,19 @@
     weighted = jnp.zeros((rank, seq), jnp.float32)
     step = d // chunks_c
     for i in range(chunks_c):
-        for copy in copies[i]:
-            copy.wait()
+        arrived(i)
         cols = pl.ds(i * step, step)
         weighted += lax.dot_general(pm_v[:, cols], c_v[:, cols], NT, preferred_element_type=jnp.float32)
     hidden_low = jnp.zeros((rank, seq), jnp.float32)
     step = ff // chunks_h
     for i in range(chunks_h):
-        for copy in copies[chunks_c + i]:
-            copy.wait()
+        arrived(chunks_c + i)
         cols = pl.ds(i * step, step)
         hidden_low += lax.dot_general(ph_v[:, cols], h_v[:, cols], NT, preferred_element_type=jnp.float32)
 
-    maskf = mask[...].astype(jnp.float32)
+    for copy in small:
+        copy.wait()
+    maskf = m_v[...].astype(jnp.float32)
     both = jnp.concatenate([hidden_low, weighted], axis=0) * maskf
     gram = lax.dot_general(both, both, NT, precision=HIGHEST, preferred_element_type=jnp.float32)
     row = lax.broadcasted_iota(jnp.int32, (rank, 2 * rank), 0)
@@ -151,21 +168,30 @@
     grad = jnp.where(first, 0.0, gram[:rank]) * (1.0 / seq**0.5)
     twice = grad + pltpu.roll(grad, rank, 1)
     half = rank // 2
-    place = hi + high * ((low // 4) % 2) + 2 * high * ((low // 2) % 2) + 4 * high * (low % 2)
-    g[place] = jnp.where(first[:half], twice[:half], twice[half:])
+    folded = jnp.where(first[:half], twice[:half], twice[half:])
+    b4, b2, b1 = low // 4 % 2, low // 2 % 2, low % 2
+    place_a = hi + high * (b4 + 2 * b2 + 4 * b1)
+    place_b = hi + high * (b2 + 2 * b4 + 4 * b1)
+    g_a[place_a] = folded[: half // 2]
+    g_b[place_b] = folded[half // 2 :]
+    halves = ((g_a, place_a, (4, 2, 1)), (g_b, place_b, (2, 4, 1)))
 
     def g_copies(stage):
-        if stage == 0:
-            return [
-                remote(g.at[place], g.at[place], g_send.at[t - 1], g_recv.at[t - 1], in_column(t))
-                for t in range(1, high)
-            ]
-        held = high * 2 ** (stage - 1)
-        bit = PLANE // 2**stage
-        partner = me + (1 - 2 * ((me // bit) % 2)) * bit
-        span = pl.ds(pl.multiple_of(place // held * held, held), held)
-        sem = high - 2 + stage
-        return [remote(g.at[span], g.at[span], g_send.at[sem], g_recv.at[sem], partner)]
+        result = []
+        for k, (g, place, bits) in enumerate(halves):
+            if stage == 0:
+                for t in range(1, high):
+                    result.append(
+                        remote(g.at[place], g.at[place], g_send.at[k, t - 1], g_recv.at[k, t - 1], in_column(t))
+                    )
+                continue
+            held = high * 2 ** (stage - 1)
+            bit = bits[stage - 1]
+            partner = me + (1 - 2 * ((me // bit) % 2)) * bit
+            span = pl.ds(pl.multiple_of(place // held * held, held), held)
+            sem = high - 2 + stage
+            result.append(remote(g.at[span], g.at[span], g_send.at[k, sem], g_recv.at[k, sem], partner))
+        return result
 
     stages = [start(g_copies(0))]
 
@@ -190,7 +216,6 @@
         remote(red, zr.at[t - 1], z_send.at[t - 1], z_recv.at[t - 1], in_column(t))
         for t in range(1, high)
     ])
-    next_stage()
     for copy in to_column:
         copy.wait_recv()
     for t in range(high - 1):
@@ -200,6 +225,7 @@
         remote(fs.at[low], fs.at[low], ag_send.at[t - 1], ag_recv.at[t - 1], in_plane(t))
         for t in range(1, PLANE)
     ])
+    next_stage()
     for copy in shares:
         copy.wait_recv()
     next_stage()
@@ -208,7 +234,7 @@
     twin = jnp.sum(jnp.where((row == 0) & (lane == 1), total, 0.0), keepdims=True)
     total = jnp.where(spare, twin, total)
     for i, inverse in enumerate(inverses(total / counted)):
-        if i == 2:
+        if i == 5:
             next_stage()
 
     zeros = jnp.zeros((rank, 2 * rank), jnp.float32)
@@ -217,13 +243,19 @@
     precond = precond + pltpu.roll(precond, rank, 1)
     precond = jnp.where(first[:half], precond[:half], precond[half:])
     next_stage()
-    terms = g[...] * precond[None]
-    terms = jnp.sum(terms.reshape(n, half // 8, 8, 2 * rank), axis=1).reshape(n * 8, 2 * rank)
-    sums = jnp.sum(terms, axis=1, keepdims=True)
+    def terms(g, part):
+        products = g[...] * part[None]
+        return jnp.sum(products.reshape(n, half // 16, 8, 2 * rank), axis=1)
+
+    two = terms(g_b, precond[half // 2 :])
+    order = (0, 2, 1, 3, 4, 6, 5, 7)
+    two = jnp.concatenate([two[k * high : (k + 1) * high] for k in order], axis=0)
+    sums = (terms(g_a, precond[: half // 2]) + two).reshape(n * 8, 2 * rank)
+    sums = jnp.sum(sums, axis=1, keepdims=True)
     nquery = scores_out.shape[1]
     at = lax.broadcasted_iota(jnp.int32, (n * 8, nquery), 0) // 8
     index = at % high * 8 + at // high % 2 * 4 + at // (2 * high) % 2 * 2 + at // (4 * high)
-    scores_out[...] = jnp.sum(jnp.where(index == queries[...], sums, 0.0), axis=0, keepdims=True)
+    scores_out[...] = jnp.sum(jnp.where(index == q_v[...], sums, 0.0), axis=0, keepdims=True)
     for copy in started:
         copy.wait_send()
 
@@ -246,32 +278,35 @@
             jax.ShapeDtypeStruct((rank // 2, 2 * rank), f32),
             jax.ShapeDtypeStruct((1, nquery), f32),
         ),
-        in_specs=[hbm, hbm, vmem, hbm, hbm, vmem],
+        in_specs=[hbm] * 6,
         out_specs=(vmem, vmem),
         scratch_shapes=[
             pltpu.VMEM((seq, ff), jnp.bfloat16),
             pltpu.VMEM((seq, d), jnp.bfloat16),
             pltpu.VMEM((rank, ff), jnp.bfloat16),
             pltpu.VMEM((rank, d), jnp.bfloat16),
+            pltpu.VMEM((1, seq), jnp.int32),
+            pltpu.VMEM((1, nquery), jnp.int32),
             pltpu.VMEM((rank, 2 * rank), f32),
             pltpu.VMEM((PLANE, rows, 2 * rank), f32),
             pltpu.VMEM((PLANE - 1, rows, 2 * rank), f32),
             pltpu.VMEM((rows, 2 * rank), f32),
             pltpu.VMEM((high - 1, rows, 2 * rank), f32),
             pltpu.VMEM((PLANE, rows, 2 * rank), f32),
-            pltpu.VMEM((n, rank // 2, 2 * rank), f32),
-            sem((2 * (chunks_h + chunks_c),)),
+            pltpu.VMEM((n, rank // 4, 2 * rank), f32),
+            pltpu.VMEM((n, rank // 4, 2 * rank), f32),
+            sem((2 * (chunks_h + chunks_c) + 2,)),
             sem((PLANE - 1,)),
             sem((PLANE - 1,)),
             sem((high - 1,)),
             sem((high - 1,)),
             sem((PLANE - 1,)),
             sem((PLANE - 1,)),
-            sem((high + 2,)),
-            sem((high + 2,)),
+            sem((2, high + 2)),
+            sem((2, high + 2)),
         ],
         compiler_params=pltpu.CompilerParams(
-            collective_id=0, has_side_effects=True, vmem_limit_bytes=48 * 2**20
+            collective_id=0, has_side_effects=True, vmem_limit_bytes=63 * 2**20
         ),
     )(hidden, cotangent, loss_mask, project_hidden.T, project_model.T, queries.reshape(1, nquery))
     return grads.reshape(1, rank * rank), scores

time: 35.4 us -> 31.1 us (0.88)
  local copies, waits for them, and re-layouts: 6.58 us -> 2.46 us
    unnamed x12 -> x2, local copies, waits for them, and re-layouts: 6.58 us -> 2.46 us
where the time goes in v2:
time: 31.1 us; the launch traced here: 30.8 us
  Pallas kernels  27.7 us (89%)
  local copies, waits for them, and re-layouts  2.46 us (8%)
  between operations  0.64 us (2%)
    pallas_call x1, Pallas kernels, local(): pl.pallas_call(functools.partial(kernel, n, chunks_h, chunks_c), out_shap...  27.7 us
    unnamed x2, local copies, waits for them, and re-layouts  2.46 us

profile of v2, /device:TPU:1, one launch (start us, length us, event | category | flops | bytes accessed | tf_op | source)
XLA Modules:
  0.0 30.8 jit_solution(3724127123945005656)
XLA Ops:
  0.6 27.7 %shard_map.77 = (f32[32,128]{1,0:T(8,128)}, f32[1,32]{1,0:T(1,128)}) custom-call(bf16[1,256,14336]{2,1,0:T(8,128)(2,1)} %hidden.1, bf16[1,256,4096]{2,1,0:T(8,128)(2,1)} %cot.1, s32[1,256]{1,0:T(1,128)} %mask.1, bf16[64,14336]{1,0:T(8,128)(2,1)} %bitcast.4, bf16[64,4096]{1,0:T(8,128)(2,1)} %bitcast.5, s32[1,32]{1,0:T(1,128)} %bitcast.7), custom_call_target="tpu_custom_call" | custom-call | tf_op jit(solution)/shard_map/pallas_call | solution.py:275
  28.3 1.3 %copy.10 = f32[1,4096]{1,0:T(1,128)} copy(f32[1,4096]{1,0:T(1,128)} %bitcast.6) | data formatting | bytes 32768
  29.7 1.1 %copy.11 = f32[1,32]{1,0:T(1,128)} copy(f32[1,32]{1,0:T(1,128)} %get-tuple-element.9) | data formatting | bytes 256

commit v3 on v2

--- a/solution.py
+++ b/solution.py
@@ -216,6 +216,7 @@
         remote(red, zr.at[t - 1], z_send.at[t - 1], z_recv.at[t - 1], in_column(t))
         for t in range(1, high)
     ])
+    next_stage()
     for copy in to_column:
         copy.wait_recv()
     for t in range(high - 1):
@@ -225,16 +226,14 @@
         remote(fs.at[low], fs.at[low], ag_send.at[t - 1], ag_recv.at[t - 1], in_plane(t))
         for t in range(1, PLANE)
     ])
-    next_stage()
     for copy in shares:
         copy.wait_recv()
-    next_stage()
     total = fs[...].reshape(rank, 2 * rank)
     counted = jnp.maximum(jnp.sum(jnp.where(spare, total, 0.0), keepdims=True), 1.0)
     twin = jnp.sum(jnp.where((row == 0) & (lane == 1), total, 0.0), keepdims=True)
     total = jnp.where(spare, twin, total)
     for i, inverse in enumerate(inverses(total / counted)):
-        if i == 5:
+        if i in (0, 5):
             next_stage()
 
     zeros = jnp.zeros((rank, 2 * rank), jnp.float32)
@@ -258,6 +257,17 @@
     scores_out[...] = jnp.sum(jnp.where(index == q_v[...], sums, 0.0), axis=0, keepdims=True)
     for copy in started:
         copy.wait_send()
+
+
+def finish(grads, scores, grads_out, scores_out, sem):
+    copies = [
+        pltpu.make_async_copy(grads, grads_out, sem.at[0]),
+        pltpu.make_async_copy(scores, scores_out, sem.at[1]),
+    ]
+    for copy in copies:
+        copy.start()
+    for copy in copies:
+        copy.wait()
 
 
 def local(n, hidden, cotangent, loss_mask, project_hidden, project_model, queries):
@@ -309,6 +319,17 @@
             collective_id=0, has_side_effects=True, vmem_limit_bytes=63 * 2**20
         ),
     )(hidden, cotangent, loss_mask, project_hidden.T, project_model.T, queries.reshape(1, nquery))
+    grads, scores = pl.pallas_call(
+        finish,
+        out_shape=(
+            jax.ShapeDtypeStruct(grads.shape, f32),
+            jax.ShapeDtypeStruct(scores.shape, f32),
+        ),
+        in_specs=[hbm, hbm],
+        out_specs=(hbm, hbm),
+        scratch_shapes=[sem((2,))],
+        compiler_params=pltpu.CompilerParams(vmem_limit_bytes=63 * 2**20),
+    )(grads, scores)
     return grads.reshape(1, rank * rank), scores
 
 

time: 31.1 us -> 32 us (1.029)
  Pallas kernels: 27.7 us -> 31.2 us
  local copies, waits for them, and re-layouts: 2.46 us -> 0 us
    unnamed x2 -> x0, local copies, waits for them, and re-layouts: 2.46 us -> none
    pallas_call x1, Pallas kernels: 27.7 us -> 29.6 us  [local(): pl.pallas_call(functools.partial(kernel, n, chunks_h, chunks_c), out_shap...]
    pallas_call x0 -> x1, Pallas kernels: none -> 1.63 us  [local(): pl.pallas_call(finish, out_shape=(jax.ShapeDtypeStruct(grads.shape, f32),...]
where the time goes in v3:
time: 32 us; the launch traced here: 31.8 us
  Pallas kernels  31.2 us (98%)
  between operations  0.64 us (2%)
    pallas_call x1, Pallas kernels, local(): pl.pallas_call(functools.partial(kernel, n, chunks_h, chunks_c), out_shap...  29.6 us
    pallas_call x1, Pallas kernels, local(): pl.pallas_call(finish, out_shape=(jax.ShapeDtypeStruct(grads.shape, f32),...  1.63 us

profile of v3, /device:TPU:1, one launch (start us, length us, event | category | flops | bytes accessed | tf_op | source)
XLA Modules:
  0.0 31.8 jit_solution(6212929654500950926)
XLA Ops:
  0.6 29.6 %shard_map.77 = (f32[32,128]{1,0:T(8,128)}, f32[1,32]{1,0:T(1,128)}) custom-call(bf16[1,256,14336]{2,1,0:T(8,128)(2,1)} %hidden.1, bf16[1,256,4096]{2,1,0:T(8,128)(2,1)} %cot.1, s32[1,256]{1,0:T(1,128)} %mask.1, bf16[64,14336]{1,0:T(8,128)(2,1)} %bitcast.4, bf16[64,4096]{1,0:T(8,128)(2,1)} %bitcast.5, s32[1,32]{1,0:T(1,128)} %bitcast.6), custom_call_target="tpu_custom_call" | custom-call | tf_op jit(solution)/shard_map/pallas_call | solution.py:285
  30.2 1.6 %shard_map.78 = (f32[32,128]{1,0:T(8,128)}, f32[1,32]{1,0:T(1,128)}) custom-call(f32[32,128]{1,0:T(8,128)} %get-tuple-element.6.grads, f32[1,32]{1,0:T(1,128)} %get-tuple-element.7.scores), custom_call_target="tpu_custom_call" | custom-call | tf_op jit(solution)/shard_map/pallas_call | solution.py:322

commit v4 on v3

--- a/solution.py
+++ b/solution.py
@@ -216,7 +216,6 @@
         remote(red, zr.at[t - 1], z_send.at[t - 1], z_recv.at[t - 1], in_column(t))
         for t in range(1, high)
     ])
-    next_stage()
     for copy in to_column:
         copy.wait_recv()
     for t in range(high - 1):
@@ -226,14 +225,16 @@
         remote(fs.at[low], fs.at[low], ag_send.at[t - 1], ag_recv.at[t - 1], in_plane(t))
         for t in range(1, PLANE)
     ])
+    next_stage()
     for copy in shares:
         copy.wait_recv()
+    next_stage()
     total = fs[...].reshape(rank, 2 * rank)
     counted = jnp.maximum(jnp.sum(jnp.where(spare, total, 0.0), keepdims=True), 1.0)
     twin = jnp.sum(jnp.where((row == 0) & (lane == 1), total, 0.0), keepdims=True)
     total = jnp.where(spare, twin, total)
     for i, inverse in enumerate(inverses(total / counted)):
-        if i in (0, 5):
+        if i == 5:
             next_stage()
 
     zeros = jnp.zeros((rank, 2 * rank), jnp.float32)

time: 32 us -> 30.1 us (0.941)
  Pallas kernels: 31.2 us -> 29.3 us
    pallas_call x1, Pallas kernels: 29.6 us -> 27.7 us  [local(): pl.pallas_call(functools.partial(kernel, n, chunks_h, chunks_c), out_shap...]
where the time goes in v4:
time: 30.1 us; the launch traced here: 30 us
  Pallas kernels  29.3 us (97%)
  between operations  0.64 us (2%)
    pallas_call x1, Pallas kernels, local(): pl.pallas_call(functools.partial(kernel, n, chunks_h, chunks_c), out_shap...  27.7 us
    pallas_call x1, Pallas kernels, local(): pl.pallas_call(finish, out_shape=(jax.ShapeDtypeStruct(grads.shape, f32),...  1.63 us

profile of v4, /device:TPU:1, one launch (start us, length us, event | category | flops | bytes accessed | tf_op | source)
XLA Modules:
  0.0 30.0 jit_solution(1984939638940023356)
XLA Ops:
  0.6 27.7 %shard_map.77 = (f32[32,128]{1,0:T(8,128)}, f32[1,32]{1,0:T(1,128)}) custom-call(bf16[1,256,14336]{2,1,0:T(8,128)(2,1)} %hidden.1, bf16[1,256,4096]{2,1,0:T(8,128)(2,1)} %cot.1, s32[1,256]{1,0:T(1,128)} %mask.1, bf16[64,14336]{1,0:T(8,128)(2,1)} %bitcast.4, bf16[64,4096]{1,0:T(8,128)(2,1)} %bitcast.5, s32[1,32]{1,0:T(1,128)} %bitcast.6), custom_call_target="tpu_custom_call" | custom-call | tf_op jit(solution)/shard_map/pallas_call | solution.py:286
  28.3 1.6 %shard_map.78 = (f32[32,128]{1,0:T(8,128)}, f32[1,32]{1,0:T(1,128)}) custom-call(f32[32,128]{1,0:T(8,128)} %get-tuple-element.6.grads, f32[1,32]{1,0:T(1,128)} %get-tuple-element.7.scores), custom_call_target="tpu_custom_call" | custom-call | tf_op jit(solution)/shard_map/pallas_call | solution.py:323
